TPU v7x, 256 devices: a whole 4x4x8 slice. The times are simulated.
256 devices in a mesh: step: 32 (over z, x), seq: 8 (over y, core).
Axes of the slice: x: 4, y: 4, z: 8, core: 2. Of those that a mesh axis runs over, the one named last changes fastest.
Arguments:
- trajectory: bfloat16 [64, 1024, 2048], P('step', 'seq'), may hold values from -8 to 8
- initial: bfloat16 [1024, 2048], P('seq'), may hold values from -6 to 6
- step_sizes: float32 [64], P('step'), may hold values from 0.02 to 0.1
- time_index: int32 [64], P('step'), may hold values from 0 to 999, as said below
- plan: float32 [1000], replicated, may hold values from 0.02 to 80
- adaln_weight: bfloat16 [256, 4096], replicated, may hold values from -0.375 to 0.375
- query_weight: bfloat16 [2048, 1024], P('step'), may hold values from -1 to 1
- key_weight: bfloat16 [2048, 1024], P('step'), may hold values from -1 to 1
- value_weight: bfloat16 [2048, 1024], P('step'), may hold values from -0.125 to 0.125
- out_weight: bfloat16 [1024, 2048], P('step'), may hold values from -3 to 3
Outputs:
- updated: float32 [64, 1024, 2048], P('step', 'seq')
Inputs may be any that keep to these rules, and one draw needn't show every extreme that they name: `time_index`: strictly decreasing along the steps; the first is 999 and the last 0.
All inputs are finite; a program needn't handle non-finite values.
Results may differ from a plain program's by a relative error of at most 0.0054.
Values may be sent and summed in bfloat16 or wider, within the bound.
No kernel may reach another device: no remote copies, remote signals or barrier semaphores. Data moves between devices by JAX's collectives and lax.ppermute only.
A program may use at most 128 MiB of HBM per device.

v0:
```python
import jax
import jax.numpy as jnp
from jax import lax
from jax.sharding import PartitionSpec as P

HEAD_DIM = 64


EPS = 1e-06


def entering(part, axis, combine, identity):
    place = lax.axis_index(axis)
    gathered = lax.all_gather(part, axis)
    state = jnp.zeros_like(part) + jnp.asarray(identity, part.dtype)

    def one(step, state):
        return combine(state, lax.dynamic_index_in_dim(gathered, step, 0, False))

    return lax.fori_loop(0, place, one, state)


def modulation(time_index, plan, adaln_weight):
    table_size = plan.shape[0]
    onehot = (time_index[:, None] == jnp.arange(table_size, dtype=jnp.int32)[None, :]).astype(
        jnp.float32
    )
    sigmas = jnp.sum(onehot * plan[None, :], axis=1)
    half_width = adaln_weight.shape[0] // 2
    frequency = 0.25 * jnp.exp(4.0 * jnp.arange(half_width, dtype=jnp.float32) / half_width)
    angles = jnp.log(sigmas)[:, None] * frequency[None, :]
    embedding = jnp.concatenate([jnp.cos(angles), jnp.sin(angles)], axis=1).astype(jnp.bfloat16)
    modulated = jnp.dot(embedding, adaln_weight, preferred_element_type=jnp.float32)
    feature_width = adaln_weight.shape[1] // 2
    return (modulated[:, :feature_width], modulated[:, feature_width:])


def normalize(states, shifts, scales):
    floats = states.astype(jnp.float32)
    means = jnp.mean(floats, axis=-1, keepdims=True)
    centered = floats - means
    variance = jnp.mean(centered * centered, axis=-1, keepdims=True)
    normed = centered * lax.rsqrt(variance + EPS)
    return (normed * (1.0 + scales[:, None, :]) + shifts[:, None, :]).astype(jnp.bfloat16)


def attend(queries, keys_rows, values_rows):
    step_count, length, columns = queries.shape
    head_count = columns // HEAD_DIM
    block_rows = min(512, length)
    query_heads = queries.reshape(
        step_count, length // block_rows, block_rows, head_count, HEAD_DIM
    ).transpose(1, 0, 2, 3, 4)
    key_heads = keys_rows.reshape(step_count, length, head_count, HEAD_DIM)
    value_heads = values_rows.reshape(step_count, length, head_count, HEAD_DIM)

    def one_block(query_block):
        scores = jnp.einsum(
            "sbhe,slhe->shbl", query_block, key_heads, preferred_element_type=jnp.float32
        ) * HEAD_DIM ** (-0.5)
        row_max = jnp.max(scores, axis=-1, keepdims=True)
        weights = jnp.exp(scores - row_max)
        weights = (weights / jnp.sum(weights, axis=-1, keepdims=True)).astype(jnp.bfloat16)
        return jnp.einsum(
            "shbl,slhe->sbhe", weights, value_heads, preferred_element_type=jnp.float32
        ).astype(jnp.bfloat16)

    blocks = lax.map(one_block, query_heads)
    return blocks.transpose(1, 0, 2, 3, 4).reshape(step_count, length, columns)


def add_terms(earlier, later):
    return earlier + later


def local(
    trajectory,
    initial,
    step_sizes,
    time_index,
    plan,
    adaln_weight,
    query_weight,
    key_weight,
    value_weight,
    out_weight,
):
    shifts, scales = modulation(time_index, plan, adaln_weight)
    normed = normalize(trajectory, shifts, scales)
    step_count, tok_rows, feature_width = normed.shape
    token_rows = normed.reshape(step_count * tok_rows, feature_width)
    proj_width = query_weight.shape[1]
    pieces = (
        lax.all_gather(query_weight, "step", axis=0, tiled=True),
        lax.all_gather(key_weight, "step", axis=0, tiled=True),
        lax.all_gather(value_weight, "step", axis=0, tiled=True),
    )
    selected = token_rows
    sums = tuple((jnp.dot(selected, piece, preferred_element_type=jnp.float32) for piece in pieces))
    queries, keys_rows, values_rows = [
        total_sum.astype(jnp.bfloat16).reshape(step_count, tok_rows, proj_width)
        for total_sum in sums
    ]
    heads_query, heads_key, heads_value = (
        lax.all_to_all(queries, "seq", split_axis=2, concat_axis=1, tiled=True),
        lax.all_to_all(keys_rows, "seq", split_axis=2, concat_axis=1, tiled=True),
        lax.all_to_all(values_rows, "seq", split_axis=2, concat_axis=1, tiled=True),
    )
    attended = attend(heads_query, heads_key, heads_value)
    token_out = lax.all_to_all(attended, "seq", split_axis=1, concat_axis=2, tiled=True)
    flat_out = token_out.reshape(step_count * tok_rows, proj_width)
    selected = flat_out
    drift = jnp.dot(
        selected,
        lax.all_gather(out_weight, "step", axis=0, tiled=True),
        preferred_element_type=jnp.float32,
    )
    drift = drift.reshape(step_count, tok_rows, feature_width)
    scaled = step_sizes[:, None, None] * drift
    running_sum = jnp.cumsum(scaled, axis=0)
    before = entering(running_sum[-1], "step", add_terms, jnp.zeros_like(running_sum[-1]))
    return initial.astype(jnp.float32)[None] + before[None] + running_sum


def solution(mesh):
    in_specs = (
        P("step", "seq", None),
        P("seq", None),
        P("step"),
        P("step"),
        P(),
        P(),
        P("step", None),
        P("step", None),
        P("step", None),
        P("step", None),
    )
    out_specs = P("step", "seq", None)
    return jax.shard_map(local, mesh=mesh, in_specs=in_specs, out_specs=out_specs, check_vma=False)
```

profile of v0, /device:TPU:230, one launch (start us, length us, event | category | flops | bytes accessed | tf_op | source)
XLA Modules:
  0.0 628.2 jit_solution(2338277046284447387)
XLA Ops:
  6.5 0.7 all-gather.10.cloned.1.call-update
  7.3 0.7 all-gather.8.cloned.1.call-update
  9.3 0.9 fusion.40
  10.2 1.5 convert_reduce_fusion
  11.7 1.6 fusion.34
  14.4 75.1 %all-gather.10.cloned.1.call-done = bf16[2048,1024]{1,0:T(8,128)(2,1)} async-done(((bf16[64,1024]{1,0:T(8,128)(2,1)}), bf16[2048,1024]{1,0:T(8,128)(2,1)}) %all-gather.10.cloned.1.call-update) | async-done | bytes 4194320 | tf_op jit(solution)/shard_map/all_gather | solution.py:96
  89.5 3.4 convolution_convert_fusion
  93.0 1.1 copy.44
  94.1 4.3 all-to-all-start.2
  98.4 72.9 %all-gather.8.cloned.1.call-done = bf16[2048,1024]{1,0:T(8,128)(2,1)} async-done(((bf16[64,1024]{1,0:T(8,128)(2,1)}), bf16[2048,1024]{1,0:T(8,128)(2,1)}) %all-gather.8.cloned.1.call-update) | async-done | bytes 4194320 | tf_op jit(solution)/shard_map/all_gather | solution.py:95
  171.3 3.4 convolution_convert_fusion.1
  174.8 1.1 copy.42
  175.9 4.3 all-to-all-start.1
  180.2 72.9 %all-gather.6.cloned.1.call-done = bf16[2048,1024]{1,0:T(8,128)(2,1)} async-done(((bf16[64,1024]{1,0:T(8,128)(2,1)}), bf16[2048,1024]{1,0:T(8,128)(2,1)}) %all-gather.6.cloned.1.call-update) | async-done | bytes 4194320 | tf_op jit(solution)/shard_map/all_gather | solution.py:94
  253.1 3.4 convolution_convert_fusion.2
  256.5 1.1 copy.39
  257.6 4.3 all-to-all-start
  263.2 9.1 %all-to-all-done = bf16[2,128,1024]{1,0,2:T(2,128)(2,1)S(1)} async-done(((bf16[2,128,1024]{1,0,2:T(2,128)(2,1)}), bf16[2,128,1024]{1,0,2:T(2,128)(2,1)S(1)}, u32[]{:S(2)}, u32[]{:S(2)}) %all-to-all-start) | async-done | bytes 524320 | tf_op jit(solution)/shard_map/all_to_all | solution.py:105
  273.0 19.4 %while.20 = (s32[]{:T(128)}, bf16[2,2,512,2,64]{2,4,3,1,0:T(8,128)(2,1)S(1)}, bf16[2,2,512,2,64]{2,4,3,1,0:T(8,128)(2,1)S(1)}, bf16[2,1024,2,64]{1,3,2,0:T(8,128...) while((s32[]{:T(128)}, bf16[2,2,512,2,64]{2,4,3,1,0:T(8,128)(2,1)S(1)}, ...), condition=%wide.region_6.7_spmd, body=%wide.region_3.6_spmd.sunk | while | flops 547488768 | bytes 18366548 | solution.py:68
  273.0 4.8 fusion.73
  277.8 4.9 fusion.74
  282.7 4.8 fusion.73
  287.6 4.9 fusion.74
  292.4 0.8 copy.51
  293.7 12.8 %all_to_all.60 = bf16[2,1024,128]{2,0,1:T(2,128)(2,1)S(1)} all-to-all(bf16[2,1024,128]{2,0,1:T(2,128)(2,1)S(1)} %reshape.72), channel_id=1, replica_groups=mesh['step'=32,'seq'=8] {'seq'}, dimensions={1} | all-to-all | bytes 1048576 | tf_op jit(solution)/shard_map/all_to_all | solution.py:110
  306.6 28.2 %all-gather.12.cloned.1.call-done = bf16[1024,2048]{1,0:T(8,128)(2,1)} async-done(((bf16[32,2048]{1,0:T(8,128)(2,1)}), bf16[1024,2048]{1,0:T(8,128)(2,1)}) %all-gather.12.cloned.1.call-update) | async-done | bytes 4194320 | tf_op jit(solution)/shard_map/all_gather | solution.py:115
  334.8 3.4 fusion.29
  338.2 1.3 fusion.53
  339.5 1.2 slice.14
  340.7 229.6 %all-gather.14.cloned.1.call-done = f32[32,128,2048]{2,1,0:T(8,128)} async-done(((f32[1,128,2048]{2,1,0:T(8,128)}), f32[32,128,2048]{2,1,0:T(8,128)}) %all-gather.14.cloned.1.call-update) | async-done | bytes 33554448 | tf_op jit(solution)/shard_map/all_gather | solution.py:14
  570.4 46.8 %while.21 = (s32[]{:T(128)}, f32[128,2048]{1,0:T(8,128)S(1)}, s32[]{:T(128)}, f32[32,128,2048]{2,1,0:T(8,128)}, s32[]{:T(128)}, /*index=5*/s32[]{:T(128)}, s32[]{:T(128)}) while((s32[]{:T(128)}, f32[128,2048]{1,0:T(8,128)S(1)}, s32[]{:T(128)}, f32[32,128,2048]{2,1,0:T(8,128)}, s32[]{:T(128)}, /*index=5*/s32[]{:T(128)}, s32[]{:T(128)}) %tuple.43), condition=%wide.region_9.10_spmd, body=%wide.region_8.9_spmd.sunk | while | flops 262149 | bytes 3145851 | solution.py:20
  570.4 1.5 bitcast_add_fusion.2
  571.9 1.5 bitcast_add_fusion.2
  573.4 1.5 bitcast_add_fusion.2
  574.9 1.5 bitcast_add_fusion.2
  576.5 1.5 bitcast_add_fusion.2
  578.0 1.5 bitcast_add_fusion.2
  579.5 1.5 bitcast_add_fusion.2
  581.0 1.5 bitcast_add_fusion.2
  582.5 1.5 bitcast_add_fusion.2
  584.0 1.5 bitcast_add_fusion.2
  585.5 1.5 bitcast_add_fusion.2
  587.0 1.5 bitcast_add_fusion.2
  588.5 1.5 bitcast_add_fusion.2
  590.0 1.5 bitcast_add_fusion.2
  591.6 1.5 bitcast_add_fusion.2
  593.1 1.5 bitcast_add_fusion.2
  594.6 1.5 bitcast_add_fusion.2
  596.1 1.5 bitcast_add_fusion.2
  597.6 1.5 bitcast_add_fusion.2
  599.1 1.5 bitcast_add_fusion.2
  600.6 1.5 bitcast_add_fusion.2
  602.1 1.5 bitcast_add_fusion.2
  603.6 1.5 bitcast_add_fusion.2
  605.2 1.5 bitcast_add_fusion.2
  606.7 1.5 bitcast_add_fusion.2
  608.2 1.5 bitcast_add_fusion.2
  609.7 1.5 bitcast_add_fusion.2
  611.2 1.5 bitcast_add_fusion.2
  612.7 1.5 bitcast_add_fusion.2
  614.2 1.5 bitcast_add_fusion.2
  615.7 1.5 bitcast_add_fusion.2
  617.2 1.3 convert_add_fusion
  618.5 3.1 broadcast_add_fusion
  (40 shorter events, 4.9 us)
Async XLA Ops:
  6.5 6.9 %copy-start = (bf16[256,4096]{1,0:T(8,128)(2,1)S(1)}, bf16[256,4096]{1,0:T(8,128)(2,1)}, u32[]{:S(2)}) copy-start(bf16[256,4096]{1,0:T(8,128)(2,1)} %param.19) | copy-start | bytes 6291460
  6.5 7.3 %copy-start.3 = (bf16[2,128,2048]{2,1,0:T(8,128)(2,1)S(1)}, bf16[2,128,2048]{2,1,0:T(8,128)(2,1)}, u32[]{:S(2)}) copy-start(bf16[2,128,2048]{2,1,0:T(8,128)(2,1)} %param.14) | copy-start | bytes 3145732
  6.5 83.0 %all-gather.10.cloned.1.call-start = ((), (), s32[]{:S(2)}) async-start(), calls=%async_computation.6 | async-start | bytes 4325376 | tf_op jit(solution)/shard_map/all_gather | solution.py:96
  7.3 164.1 %all-gather.8.cloned.1.call-start = ((), (), s32[]{:S(2)}) async-start(), calls=%async_computation.5 | async-start | bytes 4325376 | tf_op jit(solution)/shard_map/all_gather | solution.py:95
  8.0 245.1 %all-gather.6.cloned.1.call-start = ((), (), s32[]{:S(2)}) async-start(), calls=%async_computation.4 | async-start | bytes 4325376 | tf_op jit(solution)/shard_map/all_gather | solution.py:94
  8.7 326.0 %all-gather.12.cloned.1.call-start = ((), (), s32[]{:S(2)}) async-start(), calls=%async_computation.7 | async-start | bytes 4325376 | tf_op jit(solution)/shard_map/all_gather | solution.py:115
  94.1 81.8 %all-to-all-start.2 = ((bf16[2,128,1024]{1,0,2:T(2,128)(2,1)}), bf16[2,128,1024]{1,0,2:T(2,128)(2,1)S(1)}, u32[]{:S(2)}, u32[]{:S(2)}) async-start(bf16[2,128,1024]{1,0,2:T(2,128)(2,1)} %copy.44), calls=%async_computation.2 | async-start | bytes 1048576 | tf_op jit(solution)/shard_map/all_to_all | solution.py:107
  175.9 81.8 %all-to-all-start.1 = ((bf16[2,128,1024]{1,0,2:T(2,128)(2,1)}), bf16[2,128,1024]{1,0,2:T(2,128)(2,1)S(1)}, u32[]{:S(2)}, u32[]{:S(2)}) async-start(bf16[2,128,1024]{1,0,2:T(2,128)(2,1)} %copy.42), calls=%async_computation.1 | async-start | bytes 1048576 | tf_op jit(solution)/shard_map/all_to_all | solution.py:106
  257.6 14.6 %all-to-all-start = ((bf16[2,128,1024]{1,0,2:T(2,128)(2,1)}), bf16[2,128,1024]{1,0,2:T(2,128)(2,1)S(1)}, u32[]{:S(2)}, u32[]{:S(2)}) async-start(bf16[2,128,1024]{1,0,2:T(2,128)(2,1)} %copy.39), calls=%async_computation | async-start | bytes 1048576 | tf_op jit(solution)/shard_map/all_to_all | solution.py:105
  261.9 308.3 %all-gather.14.cloned.1.call-start = ((), (), s32[]{:S(2)}) async-start(), calls=%async_computation.8 | async-start | bytes 34603008 | tf_op jit(solution)/shard_map/all_gather | solution.py:14
  292.4 42.3 %copy-start.4 = (f32[2]{0:T(128)S(1)}, f32[2]{0:T(128)}, u32[]{:S(2)}) copy-start(f32[2]{0:T(128)} %param.16) | copy-start | bytes 28
  339.5 230.9 %copy-start.2 = (f32[2,128,2048]{2,1,0:T(8,128)}, f32[2,128,2048]{2,1,0:T(8,128)S(1)}, u32[]{:S(2)}) copy-start(f32[2,128,2048]{2,1,0:T(8,128)S(1)} %fusion.53) | copy-start | bytes 6291460
  617.2 4.5 copy-start.1
Sparse Core Ops, SparseCore 0:
  9.9 79.5 all-gather.9
  92.1 79.1 all-gather.7
  173.9 79.1 all-gather.5
  255.5 79.1 all-gather.11
  340.8 229.3 all-gather.13
where the time goes:
time: 630 us; the launch traced here: 628 us
  waiting for transfers between devices  491 us (78%)
  other arithmetic  56.5 us (9%)
  matrix products  33.5 us (5%)
  between operations  13.4 us (2%)
  starting transfers between devices  13 us (2%)
  blocking collectives  12.8 us (2%)
  local copies, waits for them, and re-layouts  7.77 us (1%)
    all_gather x1, waiting for transfers between devices, entering(): gathered = lax.all_gather(part, axis)  230 us
    all_gather x1, waiting for transfers between devices, local(): lax.all_gather(value_weight, 'step', axis=0, tiled=True)  75.1 us
    all_gather x1, waiting for transfers between devices, local(): lax.all_gather(query_weight, 'step', axis=0, tiled=True)  72.9 us
    all_gather x1, waiting for transfers between devices, local(): lax.all_gather(key_weight, 'step', axis=0, tiled=True)  72.9 us
    add x31, other arithmetic, add_terms(): return earlier + later  46.1 us
    all_gather x1, waiting for transfers between devices, local(): lax.all_gather(out_weight, 'step', axis=0, tiled=True)  28.2 us
    all_to_all x1, blocking collectives, local(): lax.all_to_all(attended, 'seq', split_axis=1, concat_axis=2, tiled=True)  12.8 us
  transfers between devices with their start and end apart: 8, of which 6 were waited for; matrix products, arithmetic and copies ran while one was open for 7% of the time, Pallas kernels for 0%

commit v1 on v0

v1 whole, which is shorter than its diff:
```python
import functools

import jax
import jax.numpy as jnp
from jax import lax
from jax.experimental import pallas as pl
from jax.experimental.pallas import tpu as pltpu
from jax.sharding import PartitionSpec as P

HEAD_DIM = 64
EPS = 1e-06
BF16 = jnp.bfloat16
F32 = jnp.float32
MIB = 1024 * 1024
VMEM = pl.BlockSpec(memory_space=pltpu.VMEM)
SMEM = pl.BlockSpec(memory_space=pltpu.SMEM)


def modulation(time_index, plan, adaln_weight):
    table_size = plan.shape[0]
    onehot = (time_index[:, None] == jnp.arange(table_size, dtype=jnp.int32)[None, :]).astype(F32)
    sigmas = jnp.sum(onehot * plan[None, :], axis=1)
    half_width = adaln_weight.shape[0] // 2
    frequency = 0.25 * jnp.exp(4.0 * jnp.arange(half_width, dtype=F32) / half_width)
    angles = jnp.log(sigmas)[:, None] * frequency[None, :]
    embedding = jnp.concatenate([jnp.cos(angles), jnp.sin(angles)], axis=1).astype(BF16)
    modulated = jnp.dot(embedding, adaln_weight, preferred_element_type=F32)
    feature_width = adaln_weight.shape[1] // 2
    return (modulated[:, :feature_width], modulated[:, feature_width:])


def project_kernel(mine_ref, other_ref, shift_ref, gain_ref, weight_ref, out_ref, normed_ref):
    rows = mine_ref.shape[0]
    for part, ref in enumerate((mine_ref, other_ref)):
        floats = ref[...].astype(F32)
        centered = floats - jnp.mean(floats, axis=-1, keepdims=True)
        variance = jnp.mean(centered * centered, axis=-1, keepdims=True)
        normed = centered * lax.rsqrt(variance + EPS)
        normed_ref[part * rows : (part + 1) * rows, :] = (
            normed * gain_ref[...] + shift_ref[...]
        ).astype(BF16)
    out_ref[...] = jnp.dot(
        normed_ref[...], weight_ref[...], preferred_element_type=F32
    ).astype(BF16)


def project(mine, other, shift, gain, weight):
    rows, width = mine.shape
    columns = weight.shape[1]
    return pl.pallas_call(
        project_kernel,
        out_shape=jax.ShapeDtypeStruct((2 * rows, columns), BF16),
        in_specs=[VMEM] * 5,
        out_specs=VMEM,
        scratch_shapes=[pltpu.VMEM((2 * rows, width), BF16)],
        compiler_params=pltpu.CompilerParams(vmem_limit_bytes=24 * MIB),
        cost_estimate=pl.CostEstimate(
            flops=4 * rows * width * columns,
            bytes_accessed=4 * rows * width + 2 * width * columns,
            transcendentals=0,
        ),
        name="project",
    )(mine, other, shift, gain, weight)


def attend_kernel(place_ref, *refs):
    parts = refs[:4]
    out_ref, keys_ref, values_ref = refs[4:]
    rows = parts[0].shape[0]
    pair = 2 * HEAD_DIM
    for position, part in enumerate(parts):
        span = slice(position * rows, (position + 1) * rows)
        keys_ref[span, :] = part[:, pair : 2 * pair]
        values_ref[span, :pair] = part[:, 2 * pair :]
    values_ref[:, pair:] = jnp.ones((4 * rows, pair), BF16)
    first = lax.broadcasted_iota(jnp.int32, (1, pair), 1) < HEAD_DIM
    scale = HEAD_DIM ** (-0.5)
    half = rows // 2
    for position, part in enumerate(parts):
        queries = part[:, :pair].astype(F32) * scale
        heads = []
        for mask in (first, jnp.logical_not(first)):
            chosen = jnp.where(mask, queries, 0.0).astype(BF16)
            scores = lax.dot_general(
                chosen, keys_ref[...], (((1,), (1,)), ((), ())), preferred_element_type=F32
            )
            weights = jnp.exp(scores - jnp.max(scores, axis=-1, keepdims=True)).astype(BF16)
            summed = jnp.dot(weights, values_ref[...], preferred_element_type=F32)
            heads.append(summed[:, :pair] / summed[:, pair:])
        attended = jnp.where(first, heads[0], heads[1]).astype(BF16)
        out_ref[place_ref[2 * position]] = attended[:half]
        out_ref[place_ref[2 * position + 1]] = attended[half:]


def attend(place, parts):
    rows = parts[0].shape[0]
    pair = 2 * HEAD_DIM
    return pl.pallas_call(
        attend_kernel,
        out_shape=jax.ShapeDtypeStruct((8, rows // 2, pair), BF16),
        in_specs=[SMEM] + [VMEM] * 4,
        out_specs=VMEM,
        scratch_shapes=[pltpu.VMEM((4 * rows, pair), BF16), pltpu.VMEM((4 * rows, 2 * pair), BF16)],
        compiler_params=pltpu.CompilerParams(vmem_limit_bytes=32 * MIB),
        cost_estimate=pl.CostEstimate(
            flops=16 * 16 * rows * rows * pair,
            bytes_accessed=8 * rows * 3 * pair,
            transcendentals=2 * 16 * rows * rows,
        ),
        name="attend",
    )(place, *parts)


def earlier_kernel(sums_ref, out_ref):
    running = jnp.zeros(sums_ref.shape[1:], F32)
    for index in range(sums_ref.shape[0]):
        out_ref[index] = running.astype(BF16)
        running = running + sums_ref[index].astype(F32)


def earlier(sums):
    return pl.pallas_call(
        earlier_kernel,
        out_shape=jax.ShapeDtypeStruct(sums.shape, BF16),
        in_specs=[VMEM],
        out_specs=VMEM,
        name="earlier",
    )(sums)


def side_by_side(blocks_ref):
    return jnp.concatenate([blocks_ref[index] for index in range(blocks_ref.shape[0])], axis=1)


def own_kernel(sizes_ref, first_ref, second_ref, weight_ref, initial_ref, out_ref):
    rows = initial_ref.shape[0]
    both = jnp.concatenate([side_by_side(first_ref), side_by_side(second_ref)], axis=0)
    drift = jnp.dot(both, weight_ref[...], preferred_element_type=F32)
    start = initial_ref[...].astype(F32) + sizes_ref[0] * drift[:rows]
    out_ref[0] = start
    out_ref[1] = start + sizes_ref[1] * drift[rows:]


def own_terms(sizes, first, second, weight, initial):
    rows, width = initial.shape
    tile = 512
    blocks = pl.BlockSpec(first.shape, lambda n: (0, 0, 0))
    return pl.pallas_call(
        own_kernel,
        out_shape=jax.ShapeDtypeStruct((2, rows, width), F32),
        grid=(width // tile,),
        in_specs=[
            SMEM,
            blocks,
            blocks,
            pl.BlockSpec((weight.shape[0], tile), lambda n: (0, n)),
            pl.BlockSpec((rows, tile), lambda n: (0, n)),
        ],
        out_specs=pl.BlockSpec((2, rows, tile), lambda n: (0, 0, n)),
        compiler_params=pltpu.CompilerParams(vmem_limit_bytes=24 * MIB),
        cost_estimate=pl.CostEstimate(
            flops=4 * rows * weight.shape[0] * width,
            bytes_accessed=2 * weight.size + 8 * rows * width,
            transcendentals=0,
        ),
        name="own_terms",
    )(sizes, first, second, weight, initial)


def total_kernel(before_ref, weight_ref, own_ref, out_ref):
    drift = jnp.dot(side_by_side(before_ref), weight_ref[...], preferred_element_type=F32)
    out_ref[0] = own_ref[0] + drift
    out_ref[1] = own_ref[1] + drift


def totals(before, weight, own):
    _, rows, width = own.shape
    tile = 512
    return pl.pallas_call(
        total_kernel,
        out_shape=jax.ShapeDtypeStruct(own.shape, F32),
        grid=(width // tile,),
        in_specs=[
            pl.BlockSpec(before.shape, lambda n: (0, 0, 0)),
            pl.BlockSpec((weight.shape[0], tile), lambda n: (0, n)),
            pl.BlockSpec((2, rows, tile), lambda n: (0, 0, n)),
        ],
        out_specs=pl.BlockSpec((2, rows, tile), lambda n: (0, 0, n)),
        compiler_params=pltpu.CompilerParams(vmem_limit_bytes=24 * MIB),
        name="totals",
    )(before, weight, own)


def local(
    trajectory,
    initial,
    step_sizes,
    time_index,
    plan,
    adaln_weight,
    query_weight,
    key_weight,
    value_weight,
    out_weight,
):
    groups = lax.axis_size("step")
    fields = lax.axis_size("seq")
    chips = fields // 2
    place = lax.axis_index("seq")
    pair = 2 * HEAD_DIM
    swap = [(i, i ^ 1) for i in range(fields)]

    out_full = lax.all_gather(out_weight, "step", axis=0, tiled=True)

    shifts_by = (1, chips - 1, 2)
    fetched = []
    for step in range(2):
        fetched.append(
            [trajectory[step]]
            + [
                lax.ppermute(
                    trajectory[step], "seq", [(i, (i + 2 * by) % fields) for i in range(fields)]
                )
                for by in shifts_by
            ]
        )
    mine = jnp.concatenate(
        [
            lax.dynamic_slice_in_dim(weight, place * pair, pair, axis=1)
            for weight in (query_weight, key_weight, value_weight)
        ],
        axis=1,
    )
    weight = lax.all_to_all(
        jnp.broadcast_to(mine[None], (groups,) + mine.shape), "step", 0, 0
    ).reshape(-1, mine.shape[1])

    shifts, scales = modulation(time_index, plan, adaln_weight)
    gains = 1.0 + scales

    chip, core = place // 2, place % 2
    source_chips = [chip] + [(chip - by) % chips for by in shifts_by]
    places = jnp.stack(
        [spot for source in source_chips for spot in (2 * source + core, 2 * source + 1 - core)]
    ).astype(jnp.int32)

    gathered = []
    for step in range(2):
        parts = []
        for block in fetched[step]:
            other = lax.ppermute(block, "seq", swap)
            parts.append(
                project(block, other, shifts[step][None], gains[step][None], weight)
            )
        attended = attend(places, parts)
        gathered.append(lax.all_to_all(attended, "seq", 0, 0))

    first, second = gathered
    sums = step_sizes[0] * first.astype(F32) + step_sizes[1] * second.astype(F32)
    slices = sums.astype(BF16).reshape(groups, -1, pair)
    before = lax.all_to_all(earlier(lax.all_to_all(slices, "step", 0, 0)), "step", 0, 0)
    own = own_terms(step_sizes, first, second, out_full, initial)
    return totals(before.reshape(first.shape), out_full, own)


def solution(mesh):
    in_specs = (
        P("step", "seq", None),
        P("seq", None),
        P("step"),
        P("step"),
        P(),
        P(),
        P("step", None),
        P("step", None),
        P("step", None),
        P("step", None),
    )
    out_specs = P("step", "seq", None)
    return jax.shard_map(local, mesh=mesh, in_specs=in_specs, out_specs=out_specs, check_vma=False)
```

time: 630 us -> 181 us (0.29)
  the two profiles are of different devices: /device:TPU:230 before, /device:TPU:1 now
where the time goes in v1:
time: 181 us; the launch traced here: 179 us
  starting transfers between devices  63 us (35%)
  Pallas kernels  38.5 us (21%)
  waiting for transfers between devices  25.1 us (14%)
  blocking collectives  19.6 us (11%)
  local copies, waits for them, and re-layouts  16.7 us (9%)
  between operations  13.8 us (8%)
    ppermute x8, starting transfers between devices, local(): other = lax.ppermute(block, 'seq', swap)  29.4 us
    pallas_call x8, Pallas kernels, project(): pl.pallas_call(project_kernel, out_shape=jax.ShapeDtypeStruct((2 * rows,...  22.8 us
    all_to_all x1, blocking collectives, local(): lax.all_to_all(slices, 'step', 0, 0)  19.6 us
    ppermute x6, waiting for transfers between devices, local(): lax.ppermute(trajectory[step], 'seq', [(i, (i + 2 * by) % fields) for i i...  14.4 us
    all_to_all x1, starting transfers between devices, local(): lax.all_to_all(jnp.broadcast_to(mine[None], (groups,) + mine.shape), 'ste...  12.1 us
    unnamed x42, local copies, waits for them, and re-layouts  11.9 us
    all_to_all x2, starting transfers between devices, local(): gathered.append(lax.all_to_all(attended, 'seq', 0, 0))  9.49 us
    pallas_call x2, Pallas kernels, attend(): pl.pallas_call(attend_kernel, out_shape=jax.ShapeDtypeStruct((8, rows //...  8.29 us
  transfers between devices with their start and end apart: 19, of which 5 were waited for; matrix products, arithmetic and copies ran while one was open for 4% of the time, Pallas kernels for 20%

profile of v1, /device:TPU:1, one launch (start us, length us, event | category | flops | bytes accessed | tf_op | source)
XLA Modules:
  0.0 178.7 jit_solution(558405498647240789)
XLA Ops:
  6.5 0.7 all-gather.2.cloned.1.call-update
  7.3 0.7 constant_dynamic-slice_fusion.2
  8.0 0.7 constant_dynamic-slice_fusion
  8.7 1.4 broadcast_in_dim.2
  10.1 12.1 %all-to-all-start = ((bf16[32,64,384]{2,1,0:T(8,128)(2,1)}), bf16[32,64,384]{2,1,0:T(8,128)(2,1)}, u32[]{:S(2)}, u32[]{:S(2)}) async-start(bf16[32,64,384]{2,1,0:T(8,128)(2,1)} %broadcast_in_dim.2), calls=%async_computation | async-start | bytes 3145728 | tf_op jit(solution)/shard_map/all_to_all | solution.py:234
  22.2 1.3 slice_bitcast_fusion.1
  23.5 1.4 collective-permute-start.1
  24.9 1.5 collective-permute-start.3
  26.4 1.6 collective-permute-start.5
  28.0 0.8 collective-permute-start.10
  28.8 1.4 collective-permute-start.12
  30.2 0.2 fusion
  30.4 0.1 fusion.1
  30.5 7.0 %collective-permute-done.1.mine_ref = bf16[128,2048]{1,0:T(8,128)(2,1)S(1)} collective-permute-done((bf16[128,2048]{1,0:T(8,128)(2,1)S(1)}, bf16[128,2048]{1,0:T(8,128)(2,1)S(1)}, u32[]{:S(2)}, u32[]{:S(2)}) %collective-permute-start.1) | collective-permute-done | bytes 524320 | tf_op jit(solution)/shard_map/ppermute | solution.py:221
  37.5 0.0 collective-permute-start.8
  37.5 0.0 collective-permute-done.3.mine_ref
  37.6 13.5 %collective-permute-start.2 = (bf16[128,2048]{1,0:T(8,128)(2,1)S(1)}, bf16[128,2048]{1,0:T(8,128)(2,1)S(1)}, u32[]{:S(2)}, u32[]{:S(2)}) collective-permute-start(bf16[128,2048]{1,0:T(8,128)(2,1)S(1)} %collective-permute-done.1.mine_ref), channel_id=1, source_target_pairs={{0,1},{1,0},{2,3},{3,2},{4,5},{5,4},{6,7},{7,6},{8,9},{9,8},{10,11... | collective-permute-start | bytes 1572872 | tf_op jit(solution)/shard_map/ppermute | solution.py:251
  51.1 2.1 %collective-permute-start.4 = (bf16[128,2048]{1,0:T(8,128)(2,1)S(1)}, bf16[128,2048]{1,0:T(8,128)(2,1)S(1)}, u32[]{:S(2)}, u32[]{:S(2)}) collective-permute-start(bf16[128,2048]{1,0:T(8,128)(2,1)S(1)} %collective-permute-done.3.mine_ref), channel_id=1, source_target_pairs={{0,1},{1,0},{2,3},{3,2},{4,5},{5,4},{6,7},{7,6},{8,9},{9,8},{10,11... | collective-permute-start | bytes 1572872 | tf_op jit(solution)/shard_map/ppermute | solution.py:251
  53.2 6.5 %collective-permute-done.10.mine_ref = bf16[128,2048]{1,0:T(8,128)(2,1)} collective-permute-done((bf16[128,2048]{1,0:T(8,128)(2,1)S(1)}, bf16[128,2048]{1,0:T(8,128)(2,1)}, u32[]{:S(2)}, u32[]{:S(2)}) %collective-permute-start.10) | collective-permute-done | bytes 524320 | tf_op jit(solution)/shard_map/ppermute | solution.py:221
  59.7 12.6 %collective-permute-start.6 = (bf16[128,2048]{1,0:T(8,128)(2,1)S(1)}, bf16[128,2048]{1,0:T(8,128)(2,1)S(1)}, u32[]{:S(2)}, u32[]{:S(2)}) collective-permute-start(bf16[128,2048]{1,0:T(8,128)(2,1)S(1)} %collective-permute-done.5.mine_ref), channel_id=1, source_target_pairs={{0,1},{1,0},{2,3},{3,2},{4,5},{5,4},{6,7},{7,6},{8,9},{9,8},{10,11... | collective-permute-start | bytes 1572872 | tf_op jit(solution)/shard_map/ppermute | solution.py:251
  72.3 0.4 fusion.3
  72.7 0.0 collective-permute-done.12.mine_ref
  72.7 0.1 collective-permute-start
  72.8 0.9 collective-permute-done.8.mine_ref
  73.7 0.5 collective-permute-start.7
  74.2 0.0 collective-permute-done.2.other_ref
  74.2 0.8 copy-done.11
  75.0 0.0 collective-permute-start.11
  75.0 0.8 copy-done.13
  75.9 0.5 collective-permute-start.13
  76.4 0.8 copy-done.15
  77.2 0.0 collective-permute-start.9
  77.3 0.1 stack.35.place_ref
  77.4 0.0 all-to-all-done
  77.4 1.0 copy-done.6
  78.5 1.1 copy-done.12
  79.5 2.8 %project.9.refs_1_ = bf16[256,384]{1,0:T(8,128)(2,1)S(1)} custom-call(bf16[128,2048]{1,0:T(8,128)(2,1)S(1)} %copy-done.6, bf16[128,2048]{1,0:T(8,128)(2,1)S(1)} %copy-done.12, f32[1,2048]{1,0:T(1,128)S(1)} %get-tuple-element.7.shift_ref, f32[1,2048]{1,0:T(1,128)S(1)} %get-tuple-element.18.gain_ref, bf16[2048,384]{1,0:T(8,128)(2,1)} %bitcast.10.weight_ref), custom_call_target="tpu_custom_call" | custom-call | flops 402653184 | bytes 2621440 | tf_op jit(solution)/shard_map/project/pallas_call | solution.py:50
  82.3 2.7 %project.10.refs_2_ = bf16[256,384]{1,0:T(8,128)(2,1)S(1)} custom-call(bf16[128,2048]{1,0:T(8,128)(2,1)S(1)} %copy-done.8, bf16[128,2048]{1,0:T(8,128)(2,1)S(1)} %copy-done.14, f32[1,2048]{1,0:T(1,128)S(1)} %get-tuple-element.7.shift_ref, f32[1,2048]{1,0:T(1,128)S(1)} %get-tuple-element.18.gain_ref, bf16[2048,384]{1,0:T(8,128)(2,1)} %bitcast.10.weight_ref), custom_call_target="tpu_custom_call" | custom-call | flops 402653184 | bytes 2621440 | tf_op jit(solution)/shard_map/project/pallas_call | solution.py:50
  85.1 2.7 %project.11.refs_3_ = bf16[256,384]{1,0:T(8,128)(2,1)S(1)} custom-call(bf16[128,2048]{1,0:T(8,128)(2,1)S(1)} %copy-done.10, bf16[128,2048]{1,0:T(8,128)(2,1)S(1)} %copy-done.16, f32[1,2048]{1,0:T(1,128)S(1)} %get-tuple-element.7.shift_ref, f32[1,2048]{1,0:T(1,128)S(1)} %get-tuple-element.18.gain_ref, bf16[2048,384]{1,0:T(8,128)(2,1)} %bitcast.10.weight_ref), custom_call_target="tpu_custom_call" | custom-call | flops 402653184 | bytes 2621440 | tf_op jit(solution)/shard_map/project/pallas_call | solution.py:50
  87.9 2.8 %project.8.refs_0_ = bf16[256,384]{1,0:T(8,128)(2,1)S(1)} custom-call(bf16[128,2048]{1,0:T(8,128)(2,1)S(1)} %get-tuple-element.5.mine_ref, bf16[128,2048]{1,0:T(8,128)(2,1)} %collective-permute-done.other_ref, f32[1,2048]{1,0:T(1,128)S(1)} %get-tuple-element.7.shift_ref, f32[1,2048]{1,0:T(1,128)S(1)} %get-tuple-element.18.gain_ref, ...), custom_call_target="tpu_custom_call" | custom-call | flops 402653184 | bytes 2621440 | tf_op jit(solution)/shard_map/project/pallas_call | solution.py:50
  90.7 4.1 %attend.2 = bf16[8,128,128]{2,1,0:T(8,128)(2,1)} custom-call(s32[8]{0:T(128)S(1)} %stack.35.place_ref, bf16[256,384]{1,0:T(8,128)(2,1)S(1)} %project.8.refs_0_, bf16[256,384]{1,0:T(8,128)(2,1)S(1)} %project.9.refs_1_, bf16[256,384]{1,0:T(8,128)(2,1)S(1)} %project.10.refs_2_, bf16[256,384]{1,0:T(8,128)(2,1)S(1)} %project.11.refs_3_), custom_call_target="tpu_custom_call" | custom-call | flops 2147483648 | bytes 786432 | tf_op jit(solution)/shard_map/attend/pallas_call | solution.py:98
  94.9 4.5 %all-to-all-start.1 = ((bf16[8,128,128]{2,1,0:T(8,128)(2,1)}), bf16[8,128,128]{2,1,0:T(8,128)(2,1)S(1)}, u32[]{:S(2)}, u32[]{:S(2)}) async-start(bf16[8,128,128]{2,1,0:T(8,128)(2,1)} %attend.2), calls=%async_computation.1 | async-start | bytes 524288 | tf_op jit(solution)/shard_map/all_to_all | solution.py:256
  99.4 3.0 %project.14.refs_2_ = bf16[256,384]{1,0:T(8,128)(2,1)S(1)} custom-call(bf16[128,2048]{1,0:T(8,128)(2,1)} %collective-permute-done.10.mine_ref, bf16[128,2048]{1,0:T(8,128)(2,1)} %collective-permute-done.11.other_ref, f32[1,2048]{1,0:T(1,128)S(1)} %get-tuple-element.8.shift_ref, f32[1,2048]{1,0:T(1,128)S(1)} %get-tuple-element.17.gain_ref, ...), custom_call_target="tpu_custom_call" | custom-call | flops 402653184 | bytes 2621440 | tf_op jit(solution)/shard_map/project/pallas_call | solution.py:50
  102.4 3.0 %project.15.refs_3_ = bf16[256,384]{1,0:T(8,128)(2,1)S(1)} custom-call(bf16[128,2048]{1,0:T(8,128)(2,1)} %collective-permute-done.12.mine_ref, bf16[128,2048]{1,0:T(8,128)(2,1)} %collective-permute-done.13.other_ref, f32[1,2048]{1,0:T(1,128)S(1)} %get-tuple-element.8.shift_ref, f32[1,2048]{1,0:T(1,128)S(1)} %get-tuple-element.17.gain_ref, ...), custom_call_target="tpu_custom_call" | custom-call | flops 402653184 | bytes 2621440 | tf_op jit(solution)/shard_map/project/pallas_call | solution.py:50
  105.4 3.0 %project.13.refs_1_ = bf16[256,384]{1,0:T(8,128)(2,1)S(1)} custom-call(bf16[128,2048]{1,0:T(8,128)(2,1)} %collective-permute-done.8.mine_ref, bf16[128,2048]{1,0:T(8,128)(2,1)} %collective-permute-done.9.other_ref, f32[1,2048]{1,0:T(1,128)S(1)} %get-tuple-element.8.shift_ref, f32[1,2048]{1,0:T(1,128)S(1)} %get-tuple-element.17.gain_ref, ...), custom_call_target="tpu_custom_call" | custom-call | flops 402653184 | bytes 2621440 | tf_op jit(solution)/shard_map/project/pallas_call | solution.py:50
  108.4 2.8 %project.12.refs_0_ = bf16[256,384]{1,0:T(8,128)(2,1)S(1)} custom-call(bf16[128,2048]{1,0:T(8,128)(2,1)S(1)} %get-tuple-element.6.mine_ref, bf16[128,2048]{1,0:T(8,128)(2,1)} %collective-permute-done.7.other_ref, f32[1,2048]{1,0:T(1,128)S(1)} %get-tuple-element.8.shift_ref, f32[1,2048]{1,0:T(1,128)S(1)} %get-tuple-element.17.gain_ref, ...), custom_call_target="tpu_custom_call" | custom-call | flops 402653184 | bytes 2621440 | tf_op jit(solution)/shard_map/project/pallas_call | solution.py:50
  111.2 0.0 copy-start.18
  111.2 4.1 %attend.3 = bf16[8,128,128]{2,1,0:T(8,128)(2,1)} custom-call(s32[8]{0:T(128)S(1)} %stack.35.place_ref, bf16[256,384]{1,0:T(8,128)(2,1)S(1)} %project.12.refs_0_, bf16[256,384]{1,0:T(8,128)(2,1)S(1)} %project.13.refs_1_, bf16[256,384]{1,0:T(8,128)(2,1)S(1)} %project.14.refs_2_, bf16[256,384]{1,0:T(8,128)(2,1)S(1)} %project.15.refs_3_), custom_call_target="tpu_custom_call" | custom-call | flops 2147483648 | bytes 786432 | tf_op jit(solution)/shard_map/attend/pallas_call | solution.py:98
  115.4 5.0 %all-to-all-start.2 = ((bf16[8,128,128]{2,1,0:T(8,128)(2,1)}), bf16[8,128,128]{2,1,0:T(8,128)(2,1)S(1)}, u32[]{:S(2)}, u32[]{:S(2)}) async-start(bf16[8,128,128]{2,1,0:T(8,128)(2,1)} %attend.3), calls=%async_computation.2 | async-start | bytes 524288 | tf_op jit(solution)/shard_map/all_to_all | solution.py:256
  120.3 0.6 fusion.10
  120.9 5.9 %all-to-all-done.2.second_ref = bf16[8,128,128]{2,1,0:T(8,128)(2,1)S(1)} async-done(((bf16[8,128,128]{2,1,0:T(8,128)(2,1)}), bf16[8,128,128]{2,1,0:T(8,128)(2,1)S(1)}, u32[]{:S(2)}, u32[]{:S(2)}) %all-to-all-start.2) | async-done | bytes 262176 | tf_op jit(solution)/shard_map/all_to_all | solution.py:256
  126.8 1.3 add_convert_fusion
  128.1 19.6 %all_to_all.25.sums_ref = bf16[32,32,128]{2,1,0:T(8,128)(2,1)} all-to-all(bf16[32,32,128]{2,1,0:T(8,128)(2,1)S(1)} %bitcast.19), channel_id=1, replica_groups=mesh['step'=32,'seq'=8] {'step'}, dimensions={0} | all-to-all | bytes 524288 | tf_op jit(solution)/shard_map/all_to_all | solution.py:261
  147.7 1.7 earlier.1
  149.4 5.4 %all-to-all-start.4 = ((bf16[32,32,128]{2,1,0:T(8,128)(2,1)}), bf16[32,32,128]{2,1,0:T(8,128)(2,1)S(1)}, u32[]{:S(2)}, u32[]{:S(2)}) async-start(bf16[32,32,128]{2,1,0:T(8,128)(2,1)} %earlier.1), calls=%async_computation.4 | async-start | bytes 524288 | tf_op jit(solution)/shard_map/all_to_all | solution.py:261
  154.8 0.0 all-gather.2.cloned.1.call-done.weight_ref
  154.8 2.2 %copy-done.1 = bf16[1024,2048]{1,0:T(8,128)(2,1)S(1)} copy-done((bf16[1024,2048]{1,0:T(8,128)(2,1)S(1)}, bf16[1024,2048]{1,0:T(8,128)(2,1)}, u32[]{:S(2)}) %copy-start.1) | copy-done | bytes 4194328
  157.0 2.8 %own_terms.1.own_ref = f32[2,128,2048]{2,1,0:T(8,128)S(1)} custom-call(f32[2]{0:T(128)S(1)} %copy-done.18, bf16[8,128,128]{2,1,0:T(8,128)(2,1)S(1)} %all-to-all-done.1.first_ref, bf16[8,128,128]{2,1,0:T(8,128)(2,1)S(1)} %all-to-all-done.2.second_ref, bf16[1024,2048]{1,0:T(8,128)(2,1)S(1)} %copy-done.1, bf16[128,2048]{1,0:T(8,128)(2,1)S(1)} %copy-done.17), custom_call_target="tpu_custom_call" | custom-call | flops 1073741824 | bytes 6291456 | tf_op jit(solution)/shard_map/own_terms/pallas_call | solution.py:148
  159.8 0.0 copy-start.3
  159.8 1.3 copy-done.3
  161.1 4.1 %all-to-all-done.4 = bf16[32,32,128]{2,1,0:T(8,128)(2,1)S(1)} async-done(((bf16[32,32,128]{2,1,0:T(8,128)(2,1)}), bf16[32,32,128]{2,1,0:T(8,128)(2,1)S(1)}, u32[]{:S(2)}, u32[]{:S(2)}) %all-to-all-start.4) | async-done | bytes 262176 | tf_op jit(solution)/shard_map/all_to_all | solution.py:261
  165.2 2.2 %copy-done.2 = bf16[1024,2048]{1,0:T(8,128)(2,1)S(1)} copy-done((bf16[1024,2048]{1,0:T(8,128)(2,1)S(1)}, bf16[1024,2048]{1,0:T(8,128)(2,1)}, u32[]{:S(2)}) %copy-start.2) | copy-done | bytes 4194328
  167.4 1.6 copy-done.4
  169.0 2.9 %totals.1 = f32[2,128,2048]{2,1,0:T(8,128)} custom-call(bf16[8,128,128]{2,1,0:T(8,128)(2,1)S(1)} %bitcast.18, bf16[1024,2048]{1,0:T(8,128)(2,1)S(1)} %copy-done.2, f32[2,128,2048]{2,1,0:T(8,128)S(1)} %copy-done.4), custom_call_target="tpu_custom_call" | custom-call | tf_op jit(solution)/shard_map/totals/pallas_call | solution.py:179
  (46 shorter events, 0.1 us)
Async XLA Ops:
  6.5 65.8 %copy-start = (bf16[256,4096]{1,0:T(8,128)(2,1)S(1)}, bf16[256,4096]{1,0:T(8,128)(2,1)}, u32[]{:S(2)}) copy-start(bf16[256,4096]{1,0:T(8,128)(2,1)} %param.15) | copy-start | bytes 6291460
  6.5 148.3 %all-gather.2.cloned.1.call-start = ((), (), s32[]{:S(2)}) async-start(), calls=%async_computation.5 | async-start | bytes 4325376 | tf_op jit(solution)/shard_map/all_gather | solution.py:213
  10.1 20.1 %copy-start.19 = (f32[1000]{0:T(1024)S(1)}, f32[1000]{0:T(1024)}, u32[]{:S(2)}) copy-start(f32[1000]{0:T(1024)} %param.14) | copy-start | bytes 12004
  10.1 20.1 %copy-start.20 = (s32[2]{0:T(128)S(1)}, s32[2]{0:T(128)}, u32[]{:S(2)}) copy-start(s32[2]{0:T(128)} %param.13) | copy-start | bytes 28
  10.1 67.3 %all-to-all-start = ((bf16[32,64,384]{2,1,0:T(8,128)(2,1)}), bf16[32,64,384]{2,1,0:T(8,128)(2,1)}, u32[]{:S(2)}, u32[]{:S(2)}) async-start(bf16[32,64,384]{2,1,0:T(8,128)(2,1)} %broadcast_in_dim.2), calls=%async_computation | async-start | bytes 3145728 | tf_op jit(solution)/shard_map/all_to_all | solution.py:234
  23.5 14.0 %collective-permute-start.1 = (bf16[128,2048]{1,0:T(8,128)(2,1)S(1)}, bf16[128,2048]{1,0:T(8,128)(2,1)S(1)}, u32[]{:S(2)}, u32[]{:S(2)}) collective-permute-start(bf16[128,2048]{1,0:T(8,128)(2,1)S(1)} %get-tuple-element.5.mine_ref), channel_id=1, source_target_pairs={{0,2},{1,3},{2,4},{3,5},{4,6},{5,7},{6,0},{7,1},{8,10},{9,11},{10,... | collective-permute-start | bytes 1572872 | tf_op jit(solution)/shard_map/ppermute | solution.py:221
  24.9 12.6 %collective-permute-start.3 = (bf16[128,2048]{1,0:T(8,128)(2,1)S(1)}, bf16[128,2048]{1,0:T(8,128)(2,1)S(1)}, u32[]{:S(2)}, u32[]{:S(2)}) collective-permute-start(bf16[128,2048]{1,0:T(8,128)(2,1)S(1)} %get-tuple-element.5.mine_ref), channel_id=1, source_target_pairs={{0,6},{1,7},{2,0},{3,1},{4,2},{5,3},{6,4},{7,5},{8,14},{9,15},{10,... | collective-permute-start | bytes 1572872 | tf_op jit(solution)/shard_map/ppermute | solution.py:221
  26.4 24.6 %collective-permute-start.5 = (bf16[128,2048]{1,0:T(8,128)(2,1)S(1)}, bf16[128,2048]{1,0:T(8,128)(2,1)S(1)}, u32[]{:S(2)}, u32[]{:S(2)}) collective-permute-start(bf16[128,2048]{1,0:T(8,128)(2,1)S(1)} %get-tuple-element.5.mine_ref), channel_id=1, source_target_pairs={{0,4},{1,5},{2,6},{3,7},{4,0},{5,1},{6,2},{7,3},{8,12},{9,13},{10,... | collective-permute-start | bytes 1572872 | tf_op jit(solution)/shard_map/ppermute | solution.py:221
  28.0 31.7 %collective-permute-start.10 = (bf16[128,2048]{1,0:T(8,128)(2,1)S(1)}, bf16[128,2048]{1,0:T(8,128)(2,1)}, u32[]{:S(2)}, u32[]{:S(2)}) collective-permute-start(bf16[128,2048]{1,0:T(8,128)(2,1)S(1)} %get-tuple-element.6.mine_ref), channel_id=1, source_target_pairs={{0,6},{1,7},{2,0},{3,1},{4,2},{5,3},{6,4},{7,5},{8,14},{9,15},{10,... | collective-permute-start | bytes 1572872 | tf_op jit(solution)/shard_map/ppermute | solution.py:221
  28.8 44.0 %collective-permute-start.12 = (bf16[128,2048]{1,0:T(8,128)(2,1)S(1)}, bf16[128,2048]{1,0:T(8,128)(2,1)}, u32[]{:S(2)}, u32[]{:S(2)}) collective-permute-start(bf16[128,2048]{1,0:T(8,128)(2,1)S(1)} %get-tuple-element.6.mine_ref), channel_id=1, source_target_pairs={{0,4},{1,5},{2,6},{3,7},{4,0},{5,1},{6,2},{7,3},{8,12},{9,13},{10,... | collective-permute-start | bytes 1572872 | tf_op jit(solution)/shard_map/ppermute | solution.py:221
  37.5 36.2 %copy-start.5 = (bf16[128,2048]{1,0:T(8,128)(2,1)}, bf16[128,2048]{1,0:T(8,128)(2,1)S(1)}, u32[]{:S(2)}) copy-start(bf16[128,2048]{1,0:T(8,128)(2,1)S(1)} %collective-permute-done.1.mine_ref) | copy-start | bytes 1572868
  37.5 36.2 %collective-permute-start.8 = (bf16[128,2048]{1,0:T(8,128)(2,1)S(1)}, bf16[128,2048]{1,0:T(8,128)(2,1)}, u32[]{:S(2)}, u32[]{:S(2)}) collective-permute-start(bf16[128,2048]{1,0:T(8,128)(2,1)S(1)} %get-tuple-element.6.mine_ref), channel_id=1, source_target_pairs={{0,2},{1,3},{2,4},{3,5},{4,6},{5,7},{6,0},{7,1},{8,10},{9,11},{10,... | collective-permute-start | bytes 1572872 | tf_op jit(solution)/shard_map/ppermute | solution.py:221
  37.6 36.7 %copy-start.7 = (bf16[128,2048]{1,0:T(8,128)(2,1)}, bf16[128,2048]{1,0:T(8,128)(2,1)S(1)}, u32[]{:S(2)}) copy-start(bf16[128,2048]{1,0:T(8,128)(2,1)S(1)} %collective-permute-done.3.mine_ref) | copy-start | bytes 1572868
  37.6 36.7 %collective-permute-start.2 = (bf16[128,2048]{1,0:T(8,128)(2,1)S(1)}, bf16[128,2048]{1,0:T(8,128)(2,1)S(1)}, u32[]{:S(2)}, u32[]{:S(2)}) collective-permute-start(bf16[128,2048]{1,0:T(8,128)(2,1)S(1)} %collective-permute-done.1.mine_ref), channel_id=1, source_target_pairs={{0,1},{1,0},{2,3},{3,2},{4,5},{5,4},{6,7},{7,6},{8,9},{9,8},{10,11... | collective-permute-start | bytes 1572872 | tf_op jit(solution)/shard_map/ppermute | solution.py:251
  51.1 24.0 %copy-start.9 = (bf16[128,2048]{1,0:T(8,128)(2,1)}, bf16[128,2048]{1,0:T(8,128)(2,1)S(1)}, u32[]{:S(2)}) copy-start(bf16[128,2048]{1,0:T(8,128)(2,1)S(1)} %collective-permute-done.5.mine_ref) | copy-start | bytes 1572868
  51.1 24.0 %collective-permute-start.4 = (bf16[128,2048]{1,0:T(8,128)(2,1)S(1)}, bf16[128,2048]{1,0:T(8,128)(2,1)S(1)}, u32[]{:S(2)}, u32[]{:S(2)}) collective-permute-start(bf16[128,2048]{1,0:T(8,128)(2,1)S(1)} %collective-permute-done.3.mine_ref), channel_id=1, source_target_pairs={{0,1},{1,0},{2,3},{3,2},{4,5},{5,4},{6,7},{7,6},{8,9},{9,8},{10,11... | collective-permute-start | bytes 1572872 | tf_op jit(solution)/shard_map/ppermute | solution.py:251
  59.7 16.7 %collective-permute-start.6 = (bf16[128,2048]{1,0:T(8,128)(2,1)S(1)}, bf16[128,2048]{1,0:T(8,128)(2,1)S(1)}, u32[]{:S(2)}, u32[]{:S(2)}) collective-permute-start(bf16[128,2048]{1,0:T(8,128)(2,1)S(1)} %collective-permute-done.5.mine_ref), channel_id=1, source_target_pairs={{0,1},{1,0},{2,3},{3,2},{4,5},{5,4},{6,7},{7,6},{8,9},{9,8},{10,11... | collective-permute-start | bytes 1572872 | tf_op jit(solution)/shard_map/ppermute | solution.py:251
  72.7 15.1 %collective-permute-start = (bf16[128,2048]{1,0:T(8,128)(2,1)S(1)}, bf16[128,2048]{1,0:T(8,128)(2,1)}, u32[]{:S(2)}, u32[]{:S(2)}) collective-permute-start(bf16[128,2048]{1,0:T(8,128)(2,1)S(1)} %get-tuple-element.5.mine_ref), channel_id=1, source_target_pairs={{0,1},{1,0},{2,3},{3,2},{4,5},{5,4},{6,7},{7,6},{8,9},{9,8},{10,11... | collective-permute-start | bytes 1572872 | tf_op jit(solution)/shard_map/ppermute | solution.py:251
  73.7 34.7 %collective-permute-start.7 = (bf16[128,2048]{1,0:T(8,128)(2,1)S(1)}, bf16[128,2048]{1,0:T(8,128)(2,1)}, u32[]{:S(2)}, u32[]{:S(2)}) collective-permute-start(bf16[128,2048]{1,0:T(8,128)(2,1)S(1)} %get-tuple-element.6.mine_ref), channel_id=1, source_target_pairs={{0,1},{1,0},{2,3},{3,2},{4,5},{5,4},{6,7},{7,6},{8,9},{9,8},{10,11... | collective-permute-start | bytes 1572872 | tf_op jit(solution)/shard_map/ppermute | solution.py:251
  74.2 0.8 copy-start.11
  75.0 24.4 %collective-permute-start.11 = (bf16[128,2048]{1,0:T(8,128)(2,1)}, bf16[128,2048]{1,0:T(8,128)(2,1)}, u32[]{:S(2)}, u32[]{:S(2)}) collective-permute-start(bf16[128,2048]{1,0:T(8,128)(2,1)} %collective-permute-done.10.mine_ref), channel_id=1, source_target_pairs={{0,1},{1,0},{2,3},{3,2},{4,5},{5,4},{6,7},{7,6},{8,9},{9,8},{10,11... | collective-permute-start | bytes 1572872 | tf_op jit(solution)/shard_map/ppermute | solution.py:251
  75.0 0.8 copy-start.13
  75.9 26.5 %collective-permute-start.13 = (bf16[128,2048]{1,0:T(8,128)(2,1)}, bf16[128,2048]{1,0:T(8,128)(2,1)}, u32[]{:S(2)}, u32[]{:S(2)}) collective-permute-start(bf16[128,2048]{1,0:T(8,128)(2,1)} %collective-permute-done.12.mine_ref), channel_id=1, source_target_pairs={{0,1},{1,0},{2,3},{3,2},{4,5},{5,4},{6,7},{7,6},{8,9},{9,8},{10,11... | collective-permute-start | bytes 1572872 | tf_op jit(solution)/shard_map/ppermute | solution.py:251
  76.4 0.8 copy-start.15
  77.2 28.2 %collective-permute-start.9 = (bf16[128,2048]{1,0:T(8,128)(2,1)}, bf16[128,2048]{1,0:T(8,128)(2,1)}, u32[]{:S(2)}, u32[]{:S(2)}) collective-permute-start(bf16[128,2048]{1,0:T(8,128)(2,1)} %collective-permute-done.8.mine_ref), channel_id=1, source_target_pairs={{0,1},{1,0},{2,3},{3,2},{4,5},{5,4},{6,7},{7,6},{8,9},{9,8},{10,11... | collective-permute-start | bytes 1572872 | tf_op jit(solution)/shard_map/ppermute | solution.py:251
  77.4 1.1 copy-start.6
  78.5 1.1 copy-start.12
  79.5 2.8 %copy-start.8 = (bf16[128,2048]{1,0:T(8,128)(2,1)S(1)}, bf16[128,2048]{1,0:T(8,128)(2,1)}, u32[]{:S(2)}) copy-start(bf16[128,2048]{1,0:T(8,128)(2,1)} %copy-done.7) | copy-start | bytes 1572868
  79.5 2.8 %copy-start.14 = (bf16[128,2048]{1,0:T(8,128)(2,1)S(1)}, bf16[128,2048]{1,0:T(8,128)(2,1)}, u32[]{:S(2)}) copy-start(bf16[128,2048]{1,0:T(8,128)(2,1)} %copy-done.13) | copy-start | bytes 1572868
  82.3 2.8 %copy-start.10 = (bf16[128,2048]{1,0:T(8,128)(2,1)S(1)}, bf16[128,2048]{1,0:T(8,128)(2,1)}, u32[]{:S(2)}) copy-start(bf16[128,2048]{1,0:T(8,128)(2,1)} %copy-done.9) | copy-start | bytes 1572868
  82.3 2.8 %copy-start.16 = (bf16[128,2048]{1,0:T(8,128)(2,1)S(1)}, bf16[128,2048]{1,0:T(8,128)(2,1)}, u32[]{:S(2)}) copy-start(bf16[128,2048]{1,0:T(8,128)(2,1)} %copy-done.15) | copy-start | bytes 1572868
  94.9 20.5 %all-to-all-start.1 = ((bf16[8,128,128]{2,1,0:T(8,128)(2,1)}), bf16[8,128,128]{2,1,0:T(8,128)(2,1)S(1)}, u32[]{:S(2)}, u32[]{:S(2)}) async-start(bf16[8,128,128]{2,1,0:T(8,128)(2,1)} %attend.2), calls=%async_computation.1 | async-start | bytes 524288 | tf_op jit(solution)/shard_map/all_to_all | solution.py:256
  111.2 9.1 %copy-start.18 = (f32[2]{0:T(128)S(1)}, f32[2]{0:T(128)}, u32[]{:S(2)}) copy-start(f32[2]{0:T(128)} %sizes_ref.1) | copy-start | bytes 28
  115.4 39.4 %copy-start.17 = (bf16[128,2048]{1,0:T(8,128)(2,1)S(1)}, bf16[128,2048]{1,0:T(8,128)(2,1)}, u32[]{:S(2)}) copy-start(bf16[128,2048]{1,0:T(8,128)(2,1)} %initial_ref.1) | copy-start | bytes 1572868
  115.4 11.5 %all-to-all-start.2 = ((bf16[8,128,128]{2,1,0:T(8,128)(2,1)}), bf16[8,128,128]{2,1,0:T(8,128)(2,1)S(1)}, u32[]{:S(2)}, u32[]{:S(2)}) async-start(bf16[8,128,128]{2,1,0:T(8,128)(2,1)} %attend.3), calls=%async_computation.2 | async-start | bytes 524288 | tf_op jit(solution)/shard_map/all_to_all | solution.py:256
  149.4 15.8 %all-to-all-start.4 = ((bf16[32,32,128]{2,1,0:T(8,128)(2,1)}), bf16[32,32,128]{2,1,0:T(8,128)(2,1)S(1)}, u32[]{:S(2)}, u32[]{:S(2)}) async-start(bf16[32,32,128]{2,1,0:T(8,128)(2,1)} %earlier.1), calls=%async_computation.4 | async-start | bytes 524288 | tf_op jit(solution)/shard_map/all_to_all | solution.py:261
  154.8 2.2 %copy-start.1 = (bf16[1024,2048]{1,0:T(8,128)(2,1)S(1)}, bf16[1024,2048]{1,0:T(8,128)(2,1)}, u32[]{:S(2)}) copy-start(bf16[1024,2048]{1,0:T(8,128)(2,1)} %all-gather.2.cloned.1.call-done.weight_ref) | copy-start | bytes 12582916
  159.8 1.3 copy-start.3
  165.2 2.2 %copy-start.2 = (bf16[1024,2048]{1,0:T(8,128)(2,1)S(1)}, bf16[1024,2048]{1,0:T(8,128)(2,1)}, u32[]{:S(2)}) copy-start(bf16[1024,2048]{1,0:T(8,128)(2,1)} %all-gather.2.cloned.1.call-done.weight_ref) | copy-start | bytes 12582916
  167.4 1.6 copy-start.4
Sparse Core Ops, SparseCore 0:
  9.9 90.2 all-gather.1
